TPU v7x, 256 devices: a whole 4x4x8 slice. The times are simulated.
256 devices in a mesh: attn: 4 (over x), exp: 32 (over z, y), rep: 2 (over core).
Axes of the slice: x: 4, y: 4, z: 8, core: 2. Of those that a mesh axis runs over, the one named last changes fastest.
Arguments:
- tokens: bfloat16 [1536, 7168], P(('attn', 'exp'), 'rep'), may hold values from -6 to 6
- routes: int32 [1536, 8], P(('attn', 'exp')), may hold values from 0 to 31, all different within a row; in each aligned block of 12 rows (0 to 11, 12 to 23, ...) at most 6 rows name the same one
- route_weights: float32 [1536, 8], P(('attn', 'exp')), may hold values from 0.2 to 1.5
- w_gate: bfloat16 [32, 7168, 2048], P('exp', None, ('attn', 'rep')), may hold values from -0.0625 to 0.0625
- w_up: bfloat16 [32, 7168, 2048], P('exp', None, ('attn', 'rep')), may hold values from -0.0625 to 0.0625
- w_down: bfloat16 [32, 2048, 7168], P('exp', ('attn', 'rep')), may hold values from -0.125 to 0.125
Outputs:
- mixed: bfloat16 [1536, 7168], P(('attn', 'exp'), 'rep')
Inputs may be any that keep to these rules, and one draw needn't show every extreme that they name: `routes`: the 8 experts of one request are distinct. Among the rows of one device no expert is chosen more than 6 times, and in some device some expert is chosen exactly 6 times.
All inputs are finite; a program needn't handle non-finite values.
Results may differ from a plain program's by a relative error of at most 0.02.
Values may be sent and summed in bfloat16 or wider, within the bound.
A program may use at most 128 MiB of HBM per device.

v0:
```python
import jax
import jax.numpy as jnp
from jax import lax
from jax.sharding import PartitionSpec as P


def expert_ffn(rows, w_gate, w_up, w_down, local_experts, capacity, n_rep):
    groups, sources, slots, width = rows.shape
    shaped = rows.reshape(groups, sources, local_experts, capacity, width)
    gate = jnp.einsum("ajlcd,ldf->ajlcf", shaped, w_gate, preferred_element_type=jnp.float32)
    up = jnp.einsum("ajlcd,ldf->ajlcf", shaped, w_up, preferred_element_type=jnp.float32)
    hidden = (jax.nn.silu(gate) * up).astype(jnp.bfloat16)
    down = w_down.reshape(local_experts, w_down.shape[1], n_rep, w_down.shape[2] // n_rep)
    return jnp.einsum("ajlcf,lfsd->asjlcd", hidden, down, preferred_element_type=jnp.float32)


def per_device(tokens, routes, route_weights, w_gate, w_up, w_down):
    n_exp = lax.axis_size("exp")
    n_attn = lax.axis_size("attn")
    n_rep = lax.axis_size("rep")
    tok_rows, top_count = routes.shape
    local_experts = w_gate.shape[0]
    expert_count = local_experts * n_exp
    capacity = min(tok_rows, max(2, 2 * tok_rows * top_count // expert_count))
    pair_count = tok_rows * top_count
    flat = routes.reshape(pair_count)
    onehot = (flat[:, None] == jnp.arange(expert_count, dtype=jnp.int32)[None, :]).astype(
        jnp.float32
    )
    pair_ids = jnp.arange(pair_count, dtype=jnp.int32)
    earlier = (pair_ids[:, None] > pair_ids[None, :]).astype(jnp.float32)
    before = jnp.dot(earlier, onehot, precision=lax.Precision.HIGHEST)
    slot = jnp.sum(onehot * before, axis=1).astype(jnp.int32)
    target = flat * capacity + slot
    slot_ids = jnp.arange(expert_count * capacity, dtype=jnp.int32)
    placing = jnp.any(
        target.reshape(tok_rows, top_count)[None, :, :] == slot_ids[:, None, None], axis=2
    ).astype(jnp.bfloat16)
    source = lax.all_gather(tokens, "rep", axis=1, tiled=True)
    buffer = jnp.dot(placing, source, preferred_element_type=jnp.float32).astype(jnp.bfloat16)
    buffer = buffer.reshape(1, n_exp, local_experts * capacity, source.shape[1])
    arrived = lax.all_to_all(buffer, "exp", split_axis=1, concat_axis=1, tiled=True)
    partial_value = expert_ffn(
        lax.all_gather(arrived, "attn", axis=0, tiled=True),
        w_gate,
        w_up,
        w_down,
        local_experts,
        capacity,
        n_rep,
    )
    half = w_down.shape[2] // n_rep
    partial_value = partial_value.reshape(n_attn * n_rep, n_exp, local_experts * capacity, half)
    summed = lax.psum_scatter(
        partial_value.astype(jnp.bfloat16), ("attn", "rep"), scatter_dimension=0, tiled=True
    )
    back = lax.all_to_all(summed, "exp", split_axis=1, concat_axis=1, tiled=True)
    back = back.reshape(expert_count * capacity, half)
    picked = back[target].astype(jnp.float32).reshape(tok_rows, top_count, half)
    mixed = jnp.sum(picked * route_weights[:, :, None], axis=1)
    return mixed.astype(jnp.bfloat16)


def solution(mesh):
    placed = (
        P(("attn", "exp"), "rep"),
        P(("attn", "exp"), None),
        P(("attn", "exp"), None),
        P("exp", None, ("attn", "rep")),
        P("exp", None, ("attn", "rep")),
        P("exp", ("attn", "rep"), None),
    )
    return jax.shard_map(
        per_device, mesh=mesh, in_specs=placed, out_specs=P(("attn", "exp"), "rep"), check_vma=False
    )
```

profile of v0, /device:TPU:32, one launch (start us, length us, event | category | flops | bytes accessed | tf_op | source)
XLA Modules:
  0.0 373.0 jit_solution(5352519943717344296)
XLA Ops:
  6.5 0.0 all-gather.2.cloned.1.call-start
  6.5 0.8 copy.27
  7.3 0.1 eq.28
  7.4 0.2 fusion.21
  7.6 0.1 convert_element_type.53
  7.7 0.1 fusion.22
  7.8 2.3 all_gather.6
  10.0 0.9 convolution_convert_fusion
  11.0 2.7 reshape.78
  13.7 96.3 %all_to_all.10 = bf16[1,32,6,7168]{3,2,0,1:T(8,128)(2,1)S(1)} all-to-all(bf16[1,32,6,7168]{3,2,0,1:T(8,128)(2,1)} %bitcast.74), channel_id=1, replica_groups=mesh['attn'=4,'exp'=32,'rep'=2] {'exp'}, dimensions={1} | all-to-all | bytes 5505024 | tf_op jit(solution)/shard_map/all_to_all | solution.py:42
  110.0 3.0 copy.30
  113.0 0.0 all-gather.2.cloned.1.call-update
  113.0 0.0 reduce-scatter.2.cloned.1.call-start
  113.1 9.2 %reshape.82 = bf16[256,2,3584]{2,1,0:T(2,128)(2,1)} reshape(bf16[1,256,7168]{2,1,0:T(8,128)(2,1)} %param.11) | data formatting | bytes 7340032 | tf_op jit(solution)/shard_map/reshape.6
  122.2 95.2 %all-gather.2.cloned.1.call-done = bf16[4,32,6,7168]{3,1,2,0:T(8,128)(2,1)} async-done(((bf16[1,32,6,7168]{3,1,2,0:T(8,128)(2,1)}), bf16[4,32,6,7168]{3,1,2,0:T(8,128)(2,1)}) %all-gather.2.cloned.1.call-update) | async-done | bytes 11010064 | tf_op jit(solution)/shard_map/all_gather | solution.py:44
  217.5 7.1 %fusion.6 = f32[4,32,1,6,256]{4,1,3,0,2:T(8,128)S(1)} fusion(bf16[4,32,6,7168]{3,1,2,0:T(8,128)(2,1)} %all-gather.2.cloned.1.call-done, bf16[1,7168,256]{2,1,0:T(8,128)(2,1)} %param.9), kind=kOutput, calls=%fused_computation.10 | convolution fusion | flops 2818572288 | bytes 15466496 | tf_op jit(solution)/shard_map/ajlcd,ldf->ajlcf/dot_general | solution.py:10
  224.5 1.3 copy-done.2
  225.8 1.0 copy-done.3
  226.9 3.1 fusion.18
  229.9 3.3 convert_bitcast_fusion
  233.2 4.7 %copy.32 = bf16[4,2,32,1,6,3584]{5,2,4,3,1,0:T(8,128)(2,1)} copy(bf16[4,2,32,1,6,3584]{5,2,1,4,0,3:T(8,128)(2,1)S(1)} %convert_bitcast_fusion) | data formatting | bytes 22020096 | tf_op jit(solution)/shard_map/convert_element_type | solution.py:55
  237.9 0.0 reduce-scatter.2.cloned.1.call-update
  238.0 0.0 copy-start.1
  238.0 68.5 %reduce-scatter.2.cloned.1.call-done = bf16[1,32,6,3584]{3,1,2,0:T(8,128)(2,1)} async-done(((bf16[8,32,6,3584]{3,1,2,0:T(8,128)(2,1)}), bf16[1,32,6,3584]{3,1,2,0:T(8,128)(2,1)}) %reduce-scatter.2.cloned.1.call-update) | async-done | bytes 1376272 | tf_op jit(solution)/shard_map/reduce_scatter | solution.py:54
  306.5 3.4 copy.33
  309.9 10.1 %all-to-all-start.1 = ((bf16[1,32,6,3584]{3,2,0,1:T(8,128)(2,1)}), bf16[1,32,6,3584]{3,2,0,1:T(8,128)(2,1)S(1)}, u32[]{:S(2)}, u32[]{:S(2)}) async-start(bf16[1,32,6,3584]{3,2,0,1:T(8,128)(2,1)} %copy.33), calls=%async_computation.2 | async-start | bytes 3670016 | tf_op jit(solution)/shard_map/all_to_all | solution.py:57
  320.0 0.1 mul.41
  320.1 0.1 copy.34
  320.2 43.3 %all-to-all-done.1 = bf16[1,32,6,3584]{3,2,0,1:T(8,128)(2,1)S(1)} async-done(((bf16[1,32,6,3584]{3,2,0,1:T(8,128)(2,1)}), bf16[1,32,6,3584]{3,2,0,1:T(8,128)(2,1)S(1)}, u32[]{:S(2)}, u32[]{:S(2)}) %all-to-all-start.1) | async-done | bytes 1376288 | tf_op jit(solution)/shard_map/all_to_all | solution.py:57
  363.5 0.5 reshape.83
  364.0 1.0 gather_fusion
  365.0 1.2 fusion.5
  (9 shorter events, 0.0 us)
Async XLA Ops:
  6.5 210.9 %all-gather.2.cloned.1.call-start = ((), (), s32[]{:S(2)}) async-start(), calls=%async_computation.3 | async-start | bytes 13762560 | tf_op jit(solution)/shard_map/all_gather | solution.py:44
  113.0 193.5 %reduce-scatter.2.cloned.1.call-start = ((), (), s32[]{:S(2)}) async-start(), calls=%async_computation.4 | async-start | bytes 12386304 | tf_op jit(solution)/shard_map/reduce_scatter | solution.py:54
  217.5 8.4 %copy-start.2 = (bf16[4,32,6,7168]{3,1,2,0:T(8,128)(2,1)S(1)}, bf16[4,32,6,7168]{3,1,2,0:T(8,128)(2,1)}, u32[]{:S(2)}) copy-start(bf16[4,32,6,7168]{3,1,2,0:T(8,128)(2,1)} %all-gather.2.cloned.1.call-done) | copy-start | bytes 33030148
  217.5 9.4 %copy-start.3 = (bf16[1,7168,256]{2,1,0:T(8,128)(2,1)S(1)}, bf16[1,7168,256]{2,1,0:T(8,128)(2,1)}, u32[]{:S(2)}) copy-start(bf16[1,7168,256]{2,1,0:T(8,128)(2,1)} %param.10) | copy-start | bytes 11010052
  226.9 3.1 copy-start
  238.0 82.1 %copy-start.1 = (f32[12,8]{0,1:T(8,128)S(1)}, f32[12,8]{0,1:T(8,128)}, u32[]{:S(2)}) copy-start(f32[12,8]{0,1:T(8,128)} %param.8) | copy-start | bytes 1156
  309.9 53.6 %all-to-all-start.1 = ((bf16[1,32,6,3584]{3,2,0,1:T(8,128)(2,1)}), bf16[1,32,6,3584]{3,2,0,1:T(8,128)(2,1)S(1)}, u32[]{:S(2)}, u32[]{:S(2)}) async-start(bf16[1,32,6,3584]{3,2,0,1:T(8,128)(2,1)} %copy.33), calls=%async_computation.2 | async-start | bytes 3670016 | tf_op jit(solution)/shard_map/all_to_all | solution.py:57
Sparse Core Ops, SparseCore 0:
  113.1 104.2 all-gather.1
  238.1 68.3 reduce-scatter.1
where the time goes:
time: 375 us; the launch traced here: 373 us
  waiting for transfers between devices  207 us (55%)
  blocking collectives  98.6 us (26%)
  local copies, waits for them, and re-layouts  27.9 us (7%)
  matrix products  14.5 us (4%)
  between operations  13.5 us (4%)
  starting transfers between devices  10.1 us (3%)
    all_to_all x1, blocking collectives, per_device(): lax.all_to_all(buffer, 'exp', split_axis=1, concat_axis=1, tiled=True)  96.3 us
    all_gather x1, waiting for transfers between devices, per_device(): lax.all_gather(arrived, 'attn', axis=0, tiled=True)  95.2 us
    reduce_scatter x1, waiting for transfers between devices, per_device(): lax.psum_scatter(partial_value.astype(jnp.bfloat16), ('attn', 'rep'), sca...  68.5 us
    all_to_all x1, waiting for transfers between devices, per_device(): lax.all_to_all(summed, 'exp', split_axis=1, concat_axis=1, tiled=True)  43.3 us
    all_to_all x1, starting transfers between devices, per_device(): lax.all_to_all(summed, 'exp', split_axis=1, concat_axis=1, tiled=True)  10.1 us
    another operation x1, local copies, waits for them, and re-layouts  9.17 us
  transfers between devices with their start and end apart: 3, of which 3 were waited for; matrix products, arithmetic and copies ran while one was open for 3% of the time, Pallas kernels for 0%

commit v1 on v0

v1 whole, which is shorter than its diff:
```python
import functools

import jax
import jax.numpy as jnp
from jax import lax
from jax.experimental import pallas as pl
from jax.experimental.pallas import tpu as pltpu
from jax.sharding import PartitionSpec as P

MESH = pl.DeviceIdType.MESH
NX, NZ, NY = 4, 8, 4
NF = 4
TOK, PAD, TOP, CAP, HID = 12, 16, 8, 6, 256
COLS = 256
ROWS = NZ * CAP
PLANE = NY * ROWS
F32, BF16 = jnp.float32, jnp.bfloat16


def mm(a, b, dims=((1,), (0,))):
    return lax.dot_general(a, b, (dims, ((), ())), preferred_element_type=F32)


def iota(shape, dim):
    return lax.broadcasted_iota(jnp.int32, shape, dim)


def sixth(n):
    return (n * 10923) >> 16


def kernel(
    tokens, routes, weights, wg_hbm, wu_hbm, wd_hbm, out,
    tok, tm, pick, mix, ysend, rows, wg, wu, wd, acc, hid,
    part, sib, xback, yback, zpart, zfar, znear, opp,
    wsem, ssem, rsem,
):
    half = tokens.shape[1]
    fw = half // NF
    x = lax.axis_index("attn")
    e = lax.axis_index("exp")
    c = lax.axis_index("rep")
    z, y = e // NY, lax.rem(e, NY)
    other = 1 - c

    def dev(dx=0, dz=0, dy=0, dc=0):
        return (
            lax.rem(x + dx + NX, NX),
            lax.rem(z + dz + NZ, NZ) * NY + lax.rem(y + dy + NY, NY),
            lax.rem(c + dc, 2),
        )

    partners = [dev(dx=1), dev(dx=-1), dev(dx=2), dev(dc=1)]
    partners += [dev(dy=d) for d in (1, 2, 3)]
    partners += [dev(dz=d) for d in (1, -1, 2, -2)]
    barrier = pltpu.get_barrier_semaphore()
    for partner in partners:
        pl.semaphore_signal(barrier, inc=1, device_id=partner, device_id_type=MESH)

    loads = [
        pltpu.make_async_copy(wg_hbm.at[0], wg, wsem.at[0]),
        pltpu.make_async_copy(wu_hbm.at[0], wu, wsem.at[1]),
    ]
    for h in range(2):
        for f in range(NF):
            loads.append(
                pltpu.make_async_copy(
                    wd_hbm.at[0, :, pl.ds(h * half + f * fw, fw)], wd.at[h, f], wsem.at[2 + h * NF + f]
                )
            )
    for load in loads:
        load.start()

    eye = (iota((PAD, TOK), 0) == iota((PAD, TOK), 1)).astype(F32).astype(BF16)
    for f in range(NF):
        tok[0, f, 0] = mm(eye, tokens[:, f * fw:(f + 1) * fw]).astype(BF16)
    col = iota((TOK, COLS), 1)
    expert = sixth(col)
    slot = col - CAP * expert
    hit = jnp.zeros((TOK, COLS), F32)
    weight = jnp.zeros((TOK, COLS), F32)
    for k in range(TOP):
        named = routes[:, k:k + 1] == expert
        hit = jnp.where(named, 1.0, hit)
        weight = jnp.where(named, weights[:, k:k + 1], weight)
    lower = (iota((TOK, TOK), 0) > iota((TOK, TOK), 1)).astype(F32).astype(BF16)
    before = mm(lower, hit.astype(BF16))
    placed = jnp.where(before == slot.astype(F32), weight, 0.0)
    tm[0, 0] = mm(eye, placed.astype(BF16)).astype(BF16)

    pl.semaphore_wait(barrier, len(partners))

    copies = {}

    def send(name, src, dst, where):
        index = len(copies)
        copy = pltpu.make_async_remote_copy(
            src_ref=src, dst_ref=dst, send_sem=ssem.at[index], recv_sem=rsem.at[index],
            device_id=where, device_id_type=MESH,
        )
        copy.start()
        copies[name] = copy

    def arrive(name):
        copies[name].wait_recv()

    def near(p, f):
        for s, j in ((1, 1), (-1, 7), (2, 2), (-2, 6)):
            if f == 0:
                send(("m", p, j), tm.at[p, 0], tm.at[p, j], dev(dz=s))
        for s, j in ((1, 1), (-1, 7), (2, 2), (-2, 6)):
            send(("z", p, f, j), tok.at[p, f, 0], tok.at[p, f, j], dev(dz=s))

    def far(p, f):
        if f == 0:
            for j in (2, 6):
                arrive(("m", p, j))
            send(("m", p, 3), tm.at[p, 2], tm.at[p, 3], dev(dz=1))
            send(("m", p, 5), tm.at[p, 6], tm.at[p, 5], dev(dz=-1))
            send(("m", p, 4), tm.at[p, 2], tm.at[p, 4], dev(dz=2))
        for j in (2, 6):
            arrive(("z", p, f, j))
        send(("z", p, f, 3), tok.at[p, f, 2], tok.at[p, f, 3], dev(dz=1))
        send(("z", p, f, 5), tok.at[p, f, 6], tok.at[p, f, 5], dev(dz=-1))
        if f % 2 == 0:
            send(("z", p, f, 4), tok.at[p, f, 2], tok.at[p, f, 4], dev(dz=2))
        else:
            send(("z", p, f, 4), tok.at[p, f, 6], tok.at[p, f, 4], dev(dz=-2))

    def matrices(p):
        for j in (1, 7, 3, 4, 5):
            arrive(("m", p, j))
        table = tm[p].reshape(NZ * PAD, COLS)
        n = iota((PLANE, COLS), 0)
        q = sixth(n)
        want = (z * NY + ((y + (q >> 3)) & 3)) * CAP + (n - CAP * q)
        chosen = (iota((PLANE, COLS), 1) == want).astype(F32).astype(BF16)
        wide = mm(chosen, table, ((1,), (1,)))
        n = iota((PLANE, NZ * PAD), 0)
        keep = (sixth(n) & 7) == (iota((PLANE, NZ * PAD), 1) >> 4)
        pick[p] = jnp.where(keep & (wide != 0.0), 1.0, 0.0).astype(BF16)
        tall = mm(table, chosen, ((1,), (1,)))
        n = iota((NZ * PAD, PLANE), 1)
        keep = (sixth(n) & 7) == (iota((NZ * PAD, PLANE), 0) >> 4)
        mix[p] = jnp.where(keep, tall, 0.0).astype(BF16)

    def base(p):
        return 0 if p == 0 else 3 * PLANE

    def choose(p, f):
        if f == 0:
            matrices(p)
        for j in (1, 7, 3, 4, 5):
            arrive(("z", p, f, j))
        got = mm(pick[p], tok[p, f].reshape(NZ * PAD, fw)).astype(BF16)
        rows[c, f, base(p):base(p) + ROWS] = got[:ROWS]
        for d in (1, 2, 3):
            ysend[p, f, d - 1] = got[d * ROWS:(d + 1) * ROWS]
            send(
                ("y", p, f, d), ysend.at[p, f, d - 1],
                rows.at[c, f, pl.ds(base(p) + d * ROWS, ROWS)], dev(dy=d),
            )

    def to_sibling(name, f, start, size):
        block = rows.at[c, f, pl.ds(start, size)]
        send(("s", name, f), block, block, dev(dc=1))

    def onward(p, f):
        for d in (1, 2, 3):
            arrive(("y", p, f, d))
        if p == 0:
            block = rows.at[c, f, pl.ds(0, PLANE)]
            send(("x", 1, f), block, rows.at[c, f, pl.ds(PLANE, PLANE)], dev(dx=1))
            send(("x", -1, f), block, rows.at[c, f, pl.ds(2 * PLANE, PLANE)], dev(dx=-1))
        to_sibling(p, f, base(p), PLANE)

    def neighbours(f):
        arrive(("x", 1, f))
        arrive(("x", -1, f))
        to_sibling("x", f, PLANE, 2 * PLANE)

    def gate_up(f, h):
        depth = pl.ds(pl.multiple_of(h * half + f * fw, 128), fw)
        for q in range(2):
            block = rows[h, f, 2 * q * PLANE:2 * (q + 1) * PLANE]
            mine = pl.ds(2 * q * PLANE, 2 * PLANE)
            acc[mine, :HID] += mm(block, wg[depth, :])
            acc[mine, HID:] += mm(block, wu[depth, :])

    for f in range(NF):
        if f == 0:
            send(("m", 1, 0), tm.at[0, 0], tm.at[1, 0], dev(dx=2))
            near(0, 0)
        send(("o", f), tok.at[0, f, 0], tok.at[1, f, 0], dev(dx=2))
    acc[...] = jnp.zeros_like(acc)
    items = [(p, f) for p in range(2) for f in range(NF)]
    near(*items[1])
    for step in range(len(items) + 2):
        if step < len(items):
            far(*items[step])
        if step + 2 < len(items):
            p, f = items[step + 2]
            if p == 1:
                if f == 0:
                    arrive(("m", 1, 0))
                arrive(("o", f))
            near(p, f)
        if 1 <= step <= len(items):
            choose(*items[step - 1])
        if step >= 2:
            p, f = items[step - 2]
            onward(p, f)
            if p == 1:
                neighbours(f)
                if f == 0:
                    loads[0].wait()
                    loads[1].wait()
                gate_up(f, c)
                if f > 0:
                    for name in (0, 1, "x"):
                        arrive(("s", name, f - 1))
                    gate_up(f - 1, other)
    for name in (0, 1, "x"):
        arrive(("s", name, NF - 1))
    gate_up(NF - 1, other)
    for q in range(4):
        mine = pl.ds(q * PLANE, PLANE)
        gate = acc[mine, :HID]
        hid[mine] = (gate / (1.0 + jnp.exp(-gate)) * acc[mine, HID:]).astype(BF16)

    for load in loads[2:]:
        load.wait()
    for f in range(NF):
        for name in (("x", 1, f), ("x", -1, f), ("s", 0, f), ("s", 1, f), ("s", "x", f)):
            copies[name].wait_send()

    def down(f, h, dst):
        def body(q, carry):
            mine = pl.ds(pl.multiple_of(q * PLANE, PLANE), PLANE)
            dst[mine] = mm(hid[mine], wd[h, f]).astype(BF16)
            return carry
        lax.fori_loop(0, 4, body, 0)

    def down_other(f):
        down(f, other, rows.at[0, f])
        send(("d", f), rows.at[0, f], sib.at[f], dev(dc=1))

    def leave(f):
        arrive(("d", f))
        for q in (1, 2, 3, 0):
            mine = pl.ds(q * PLANE, PLANE)
            part[f, mine] = (part[f, mine].astype(F32) + sib[f, mine].astype(F32)).astype(BF16)
            if q == 1:
                send(("xb", -1, f), part.at[f, mine], xback.at[f, 1], dev(dx=-1))
            if q == 2:
                send(("xb", 1, f), part.at[f, mine], xback.at[f, 0], dev(dx=1))
            if q == 3:
                back(1, f)

    def back(p, f):
        for d in (1, 2, 3):
            send(
                ("yb", p, f, d), part.at[f, pl.ds(base(p) + d * ROWS, ROWS)],
                yback.at[p, f, pl.ds((d - 1) * ROWS, ROWS)], dev(dy=-d),
            )

    def home(f):
        arrive(("xb", -1, f))
        arrive(("xb", 1, f))
        mine = pl.ds(0, PLANE)
        total = part[f, mine].astype(F32) + xback[f, 0].astype(F32) + xback[f, 1].astype(F32)
        part[f, mine] = total.astype(BF16)
        back(0, f)

    def combine(p, f):
        for d in (1, 2, 3):
            arrive(("yb", p, f, d))
        total = mm(mix[p, :, :ROWS], part[f, base(p):base(p) + ROWS])
        total += mm(mix[p, :, ROWS:], yback[p, f])
        zpart[p, f] = total.astype(BF16).reshape(NZ, PAD, fw)
        send(("zf", p, f, 3), zpart.at[p, f, 3], zfar.at[p, f, 0], dev(dz=-1))
        send(("zf", p, f, 5), zpart.at[p, f, 5], zfar.at[p, f, 1], dev(dz=1))
        send(("zf", p, f, 4), zpart.at[p, f, 4], zfar.at[p, f, 2], dev(dz=-2 if f % 2 == 0 else 2))

    def closer(p, f):
        send(("zn", p, f, 1), zpart.at[p, f, 1], znear.at[p, f, 0], dev(dz=-1))
        send(("zn", p, f, 7), zpart.at[p, f, 7], znear.at[p, f, 1], dev(dz=1))
        for j in (3, 5, 4):
            arrive(("zf", p, f, j))
        two = zpart[p, f, 2].astype(F32) + zfar[p, f, 0].astype(F32)
        six = zpart[p, f, 6].astype(F32) + zfar[p, f, 1].astype(F32)
        if f % 2 == 0:
            two += zfar[p, f, 2].astype(F32)
        else:
            six += zfar[p, f, 2].astype(F32)
        zpart[p, f, 2] = two.astype(BF16)
        zpart[p, f, 6] = six.astype(BF16)
        send(("zn", p, f, 2), zpart.at[p, f, 2], znear.at[p, f, 2], dev(dz=-2))
        send(("zn", p, f, 6), zpart.at[p, f, 6], znear.at[p, f, 3], dev(dz=2))

    def gathered(p, f):
        for j in (1, 7, 2, 6):
            arrive(("zn", p, f, j))
        total = zpart[p, f, 0].astype(F32)
        for i in range(4):
            total += znear[p, f, i].astype(F32)
        return total

    def opposite(f):
        opp[0, f] = gathered(1, f).astype(BF16)
        send(("ob", f), opp.at[0, f], opp.at[1, f], dev(dx=2))

    def finish(f):
        total = gathered(0, f)
        arrive(("ob", f))
        total += opp[1, f].astype(F32)
        out[:, f * fw:(f + 1) * fw] = total.astype(BF16)

    down_other(0)
    down(0, c, part.at[0])
    for f in range(NF):
        if f + 1 < NF:
            down_other(f + 1)
        leave(f)
        if f + 1 < NF:
            down(f + 1, c, part.at[f + 1])
    for f in range(NF):
        combine(1, f)
        if f > 0:
            closer(0, f - 1)
        home(f)
        closer(1, f)
        if f > 0:
            finish(f - 1)
        combine(0, f)
        opposite(f)
    closer(0, NF - 1)
    finish(NF - 1)
    for name, copy in copies.items():
        if name[0] not in ("x", "s"):
            copy.wait_send()


COPIES = 1 + NF + 2 * 7 + 2 * NF * 7 + 2 * NF * 3 + 2 * NF + 3 * NF + NF + 2 * NF + 2 * NF * 3 + 2 * NF * 7 + NF


def per_device(tokens, routes, route_weights, w_gate, w_up, w_down):
    half = tokens.shape[1]
    fw = half // NF
    vmem = pl.BlockSpec(memory_space=pltpu.VMEM)
    hbm = pl.BlockSpec(memory_space=pl.ANY)
    result = pl.pallas_call(
        kernel,
        out_shape=jax.ShapeDtypeStruct((PAD, half), BF16),
        in_specs=[vmem, vmem, vmem, hbm, hbm, hbm],
        out_specs=vmem,
        scratch_shapes=[
            pltpu.VMEM((2, NF, NZ, PAD, fw), BF16),
            pltpu.VMEM((2, NZ, PAD, COLS), BF16),
            pltpu.VMEM((2, PLANE, NZ * PAD), BF16),
            pltpu.VMEM((2, NZ * PAD, PLANE), BF16),
            pltpu.VMEM((2, NF, 3, ROWS, fw), BF16),
            pltpu.VMEM((2, NF, 4 * PLANE, fw), BF16),
            pltpu.VMEM((2 * half, HID), BF16),
            pltpu.VMEM((2 * half, HID), BF16),
            pltpu.VMEM((2, NF, HID, fw), BF16),
            pltpu.VMEM((4 * PLANE, 2 * HID), F32),
            pltpu.VMEM((4 * PLANE, HID), BF16),
            pltpu.VMEM((NF, 4 * PLANE, fw), BF16),
            pltpu.VMEM((NF, 4 * PLANE, fw), BF16),
            pltpu.VMEM((NF, 2, PLANE, fw), BF16),
            pltpu.VMEM((2, NF, 3 * ROWS, fw), BF16),
            pltpu.VMEM((2, NF, NZ, PAD, fw), BF16),
            pltpu.VMEM((2, NF, 3, PAD, fw), BF16),
            pltpu.VMEM((2, NF, 4, PAD, fw), BF16),
            pltpu.VMEM((2, NF, PAD, fw), BF16),
            pltpu.SemaphoreType.DMA((2 + 2 * NF,)),
            pltpu.SemaphoreType.DMA((COPIES,)),
            pltpu.SemaphoreType.DMA((COPIES,)),
        ],
        compiler_params=pltpu.CompilerParams(
            collective_id=0, has_side_effects=True, vmem_limit_bytes=60 * 1024 * 1024
        ),
        name="experts",
    )(tokens, routes, route_weights, w_gate, w_up, w_down)
    return result[:TOK]


def solution(mesh):
    placed = (
        P(("attn", "exp"), "rep"),
        P(("attn", "exp"), None),
        P(("attn", "exp"), None),
        P("exp", None, ("attn", "rep")),
        P("exp", None, ("attn", "rep")),
        P("exp", ("attn", "rep"), None),
    )
    return jax.shard_map(
        per_device, mesh=mesh, in_specs=placed, out_specs=P(("attn", "exp"), "rep"), check_vma=False
    )
```

time: 375 us -> 131 us (0.35)
  waiting for transfers between devices: 207 us -> 0 us
  Pallas kernels: 0 us -> 126 us
  blocking collectives: 98.6 us -> 0 us
  local copies, waits for them, and re-layouts: 27.9 us -> 4.28 us
  matrix products: 14.5 us -> 0 us
  between operations: 13.5 us -> 0.01 us
  starting transfers between devices: 10.1 us -> 0 us
    pallas_call x0 -> x1, Pallas kernels: none -> 126 us  [per_device(): pl.pallas_call(kernel, out_shape=jax.ShapeDtypeStruct((PAD, half), BF16),...]
    all_to_all x1 -> x0, blocking collectives: 96.3 us -> none  [per_device(): lax.all_to_all(buffer, 'exp', split_axis=1, concat_axis=1, tiled=True)]
    all_gather x1 -> x0, waiting for transfers between devices: 95.2 us -> none  [per_device(): lax.all_gather(arrived, 'attn', axis=0, tiled=True)]
    reduce_scatter x1 -> x0, waiting for transfers between devices: 68.5 us -> none  [per_device(): lax.psum_scatter(partial_value.astype(jnp.bfloat16), ('attn', 'rep'), sca...]
    all_to_all x1 -> x0, waiting for transfers between devices: 43.3 us -> none  [per_device(): lax.all_to_all(summed, 'exp', split_axis=1, concat_axis=1, tiled=True)]
    dot_general x5 -> x0, matrix products: 14.5 us -> none  [the longest x1 7.06 us: expert_ffn(): jnp.einsum('ajlcd,ldf->ajlcf', shaped, w_gate, preferred_element_type=jnp...]
    all_to_all x1 -> x0, starting transfers between devices: 10.1 us -> none  [per_device(): lax.all_to_all(summed, 'exp', split_axis=1, concat_axis=1, tiled=True)]
    another operation x1 -> x0, local copies, waits for them, and re-layouts: 9.17 us -> none
  transfers between devices with their start and end apart: 3 -> 0, of which waited for: 3 -> 0; matrix products, arithmetic and copies ran while one was open for 3% -> 0% of each run, Pallas kernels for 0% -> 0%
where the time goes in v1:
time: 131 us; the launch traced here: 130 us
  Pallas kernels  126 us (96%)
  local copies, waits for them, and re-layouts  4.28 us (3%)
    pallas_call x1, Pallas kernels, per_device(): pl.pallas_call(kernel, out_shape=jax.ShapeDtypeStruct((PAD, half), BF16),...  126 us
    unnamed x3, local copies, waits for them, and re-layouts  4.28 us

profile of v1, /device:TPU:32, one launch (start us, length us, event | category | flops | bytes accessed | tf_op | source)
XLA Modules:
  0.0 129.8 jit_solution(8914458502309952071)
XLA Ops:
  0.0 1.4 %copy.7.routes = s32[12,8]{1,0:T(8,128)} copy(s32[12,8]{0,1:T(8,128)} %param.7) | data formatting | bytes 768 | tf_op args[1]
  1.4 1.4 %copy.8.weights = f32[12,8]{1,0:T(8,128)} copy(f32[12,8]{0,1:T(8,128)} %param.8) | data formatting | bytes 768 | tf_op args[2]
  2.7 125.5 %experts.1 = bf16[16,3584]{1,0:T(8,128)(2,1)} custom-call(bf16[12,3584]{1,0:T(8,128)(2,1)} %tokens.1, s32[12,8]{1,0:T(8,128)} %copy.7.routes, f32[12,8]{1,0:T(8,128)} %copy.8.weights, bf16[1,7168,256]{2,1,0:T(8,128)(2,1)} %wg_hbm.1, bf16[1,7168,256]{2,1,0:T(8,128)(2,1)} %wu_hbm.1, bf16[1,256,7168]{2,1,0:T(8,128)(2,1)} %wd_hbm.1), custom_call_target="tpu_custom_call" | custom-call | tf_op jit(solution)/shard_map/experts/pallas_call | solution.py:352
  128.3 1.6 %copy.10 = bf16[12,3584]{1,0:T(8,128)(2,1)} copy(bf16[12,3584]{1,0:T(8,128)(2,1)} %bitcast.1) | data formatting | bytes 172032

commit v2 on v1

v2 whole, which is shorter than its diff:
```python
import functools

import jax
import jax.numpy as jnp
from jax import lax
from jax.experimental import pallas as pl
from jax.experimental.pallas import tpu as pltpu
from jax.sharding import PartitionSpec as P

MESH = pl.DeviceIdType.MESH
NX, NZ, NY = 4, 8, 4
WIDTHS = (512, 768, 768, 768, 512, 256)
NF = len(WIDTHS)
STARTS = tuple(sum(WIDTHS[:f]) for f in range(NF))
TOK, PAD, TOP, CAP, HID = 12, 16, 8, 6, 256
COLS = 256
ROWS = NZ * CAP
PLANE = NY * ROWS
F32, BF16 = jnp.float32, jnp.bfloat16


def mm(a, b, dims=((1,), (0,))):
    return lax.dot_general(a, b, (dims, ((), ())), preferred_element_type=F32)


def iota(shape, dim):
    return lax.broadcasted_iota(jnp.int32, shape, dim)


def sixth(n):
    return (n * 10923) >> 16


def kernel(
    tokens_hbm, routes_hbm, weights_hbm, wg_hbm, wu_hbm, wd_hbm, out_hbm,
    tokens, routes, weights, out, tok, tm, pick, mix, ysend, rows, wg, wu, wd, acc, hid,
    part, sib, xback, yback, zpart, zfar, znear, opp,
    isem, osem, wsem, ssem, rsem,
):
    half = tokens.shape[1]
    x = lax.axis_index("attn")
    e = lax.axis_index("exp")
    c = lax.axis_index("rep")
    z, y = e // NY, lax.rem(e, NY)
    other = 1 - c

    def dev(dx=0, dz=0, dy=0, dc=0):
        return (
            lax.rem(x + dx + NX, NX),
            lax.rem(z + dz + NZ, NZ) * NY + lax.rem(y + dy + NY, NY),
            lax.rem(c + dc, 2),
        )

    partners = [dev(dx=1), dev(dx=-1), dev(dx=2), dev(dc=1)]
    partners += [dev(dy=d) for d in (1, 2, 3)]
    partners += [dev(dz=d) for d in (1, -1, 2, -2)]
    barrier = pltpu.get_barrier_semaphore()
    for partner in partners:
        pl.semaphore_signal(barrier, inc=1, device_id=partner, device_id_type=MESH)

    inputs = [
        pltpu.make_async_copy(src, dst, isem.at[i])
        for i, (src, dst) in enumerate(((tokens_hbm, tokens), (routes_hbm, routes), (weights_hbm, weights)))
    ]
    for copy in inputs:
        copy.start()
    loads = [
        pltpu.make_async_copy(wg_hbm.at[0], wg, wsem.at[0]),
        pltpu.make_async_copy(wu_hbm.at[0], wu, wsem.at[1]),
    ]
    for h in range(2):
        for f in range(NF):
            loads.append(
                pltpu.make_async_copy(
                    wd_hbm.at[0, :, pl.ds(h * half + STARTS[f], WIDTHS[f])], wd[f].at[h], wsem.at[2 + h * NF + f]
                )
            )
    for load in loads:
        load.start()
    for copy in inputs:
        copy.wait()

    eye = (iota((PAD, TOK), 0) == iota((PAD, TOK), 1)).astype(F32).astype(BF16)
    for f in range(NF):
        tok[f][0, 0] = mm(eye, tokens[:, STARTS[f]:STARTS[f] + WIDTHS[f]]).astype(BF16)
    col = iota((TOK, COLS), 1)
    expert = sixth(col)
    slot = col - CAP * expert
    square = (iota((TOK, TOK), 0) == iota((TOK, TOK), 1)).astype(F32).astype(BF16)
    names = mm(square, routes[...].astype(F32).astype(BF16), ((1,), (1,))).astype(jnp.int32)
    gains = mm(square, weights[...].astype(BF16), ((1,), (1,)))
    hit = jnp.zeros((TOK, COLS), F32)
    weight = jnp.zeros((TOK, COLS), F32)
    for k in range(TOP):
        named = names[:, k:k + 1] == expert
        hit = jnp.where(named, 1.0, hit)
        weight = jnp.where(named, gains[:, k:k + 1], weight)
    lower = (iota((TOK, TOK), 0) > iota((TOK, TOK), 1)).astype(F32).astype(BF16)
    before = mm(lower, hit.astype(BF16))
    placed = jnp.where(before == slot.astype(F32), weight, 0.0)
    tm[0, 0] = mm(eye, placed.astype(BF16)).astype(BF16)

    pl.semaphore_wait(barrier, len(partners))

    inward, outward, whole = {}, {}, {}
    free = list(range(ssem.shape[0]))
    results = []

    def send(out_key, in_key, src, dst, where, block):
        if in_key not in inward:
            inward[in_key] = len(inward)
        if out_key not in outward:
            outward[out_key] = free.pop(0)
            whole[out_key] = block
        pltpu.make_async_remote_copy(
            src_ref=src, dst_ref=dst, send_sem=ssem.at[outward[out_key]], recv_sem=rsem.at[inward[in_key]],
            device_id=where, device_id_type=MESH,
        ).start()

    def waiter(block, sends, arrivals):
        return pltpu.make_async_remote_copy(
            src_ref=block, dst_ref=block, send_sem=ssem.at[sends], recv_sem=rsem.at[arrivals],
            device_id=partners[3], device_id_type=MESH,
        )

    def arrive(key, block):
        waiter(block, 0, inward[key]).wait_recv()

    def sent(keys):
        for key in keys:
            slot = outward.pop(key)
            waiter(whole[key], slot, 0).wait_send()
            free.append(slot)

    hops = ((1, 1, "b"), (-1, 7, "b"), (2, 2, "a"), (-2, 6, "a"))

    def near(p, f):
        if f == 0:
            for s, j, part_of in hops:
                send(("m", p), ("m" + part_of, p), tm.at[p, 0], tm.at[p, j], dev(dz=s), tm.at[p, pl.ds(0, 4)])
        for s, j, part_of in hops:
            send(
                ("z", p, f), ("z" + part_of, p, f), tok[f].at[p, 0], tok[f].at[p, j], dev(dz=s),
                tok[f].at[p, pl.ds(0, 4)],
            )

    def far(p, f):
        if f == 0:
            arrive(("ma", p), tm.at[p, pl.ds(0, 2)])
            for s, i, j in ((1, 2, 3), (-1, 6, 5), (2, 2, 4)):
                send(("mf", p), ("mb", p), tm.at[p, i], tm.at[p, j], dev(dz=s), tm.at[p, pl.ds(0, 3)])
        arrive(("za", p, f), tok[f].at[p, pl.ds(0, 2)])
        for s, i, j in ((1, 2, 3), (-1, 6, 5), (2, 2, 4) if f % 2 == 0 else (-2, 6, 4)):
            send(
                ("zf", p, f), ("zb", p, f), tok[f].at[p, i], tok[f].at[p, j], dev(dz=s),
                tok[f].at[p, pl.ds(0, 3)],
            )

    def matrices(p):
        arrive(("mb", p), tm.at[p, pl.ds(0, 5)])
        table = tm[p].reshape(NZ * PAD, COLS)
        n = iota((PLANE, COLS), 0)
        q = sixth(n)
        want = (z * NY + ((y + (q >> 3)) & 3)) * CAP + (n - CAP * q)
        chosen = (iota((PLANE, COLS), 1) == want).astype(F32).astype(BF16)
        wide = mm(chosen, table, ((1,), (1,)))
        n = iota((PLANE, NZ * PAD), 0)
        keep = (sixth(n) & 7) == (iota((PLANE, NZ * PAD), 1) >> 4)
        pick[p] = jnp.where(keep & (wide != 0.0), 1.0, 0.0).astype(BF16)
        tall = mm(table, chosen, ((1,), (1,)))
        n = iota((NZ * PAD, PLANE), 1)
        keep = (sixth(n) & 7) == (iota((NZ * PAD, PLANE), 0) >> 4)
        mix[p] = jnp.where(keep, tall, 0.0).astype(BF16)

    def base(p):
        return 0 if p == 0 else 3 * PLANE

    def choose(p, f):
        if f == 0:
            matrices(p)
        arrive(("zb", p, f), tok[f].at[p, pl.ds(0, 5)])
        got = mm(pick[p], tok[f][p].reshape(NZ * PAD, WIDTHS[f])).astype(BF16)
        rows[f][c, base(p):base(p) + ROWS] = got[:ROWS]
        for d in (1, 2, 3):
            ysend[f][p, d - 1] = got[d * ROWS:(d + 1) * ROWS]
            send(
                ("y", p, f), ("y", p, f), ysend[f].at[p, d - 1],
                rows[f].at[c, pl.ds(base(p) + d * ROWS, ROWS)], dev(dy=d), ysend[f].at[p],
            )

    def to_sibling(f, start, size):
        block = rows[f].at[c, pl.ds(start, size)]
        send(("s", f), ("s", f), block, block, dev(dc=1), rows[f].at[c])

    def from_sibling(f):
        arrive(("s", f), rows[f].at[other])

    def onward(p, f):
        arrive(("y", p, f), rows[f].at[c, pl.ds(base(p) + ROWS, 3 * ROWS)])
        if p == 0:
            block = rows[f].at[c, pl.ds(0, PLANE)]
            both_ways = rows[f].at[c, pl.ds(PLANE, 2 * PLANE)]
            send(("x", f), ("x", f), block, rows[f].at[c, pl.ds(PLANE, PLANE)], dev(dx=1), both_ways)
            send(("x", f), ("x", f), block, rows[f].at[c, pl.ds(2 * PLANE, PLANE)], dev(dx=-1), both_ways)
        to_sibling(f, base(p), PLANE)

    def neighbours(f):
        arrive(("x", f), rows[f].at[c, pl.ds(PLANE, 2 * PLANE)])
        to_sibling(f, PLANE, 2 * PLANE)

    def gate_up(f, h):
        depth = pl.ds(pl.multiple_of(h * half + STARTS[f], 128), WIDTHS[f])
        for q in range(2):
            block = rows[f][h, 2 * q * PLANE:2 * (q + 1) * PLANE]
            mine = pl.ds(2 * q * PLANE, 2 * PLANE)
            acc[mine, :HID] += mm(block, wg[depth, :])
            acc[mine, HID:] += mm(block, wu[depth, :])

    items = [(p, f) for p in range(2) for f in range(NF)]
    near(*items[0])
    send(("o", 0), ("om", 0), tm.at[0, 0], tm.at[1, 0], dev(dx=2), tm.at[0, 0])
    for f in range(NF):
        send(("oz", f), ("oz", f), tok[f].at[0, 0], tok[f].at[1, 0], dev(dx=2), tok[f].at[0, 0])
    acc[...] = jnp.zeros_like(acc)
    near(*items[1])

    def further(step):
        if step < len(items):
            far(*items[step])
        for later in (2, 3) if step == 0 else (step + 3,):
            if later < len(items):
                p, f = items[later]
                if p == 1:
                    if f == 0:
                        arrive(("om", 0), tm.at[0, 0])
                    arrive(("oz", f), tok[f].at[0, 0])
                near(p, f)

    further(0)
    further(1)
    for step in range(len(items) + 2):
        if step < len(items):
            further(step + 2)
            choose(*items[step])
        if step >= 2:
            p, f = items[step - 2]
            if p == 1 and f > 0:
                from_sibling(f - 1)
                gate_up(f - 1, other)
            onward(p, f)
            if p == 1:
                neighbours(f)
                if f == 0:
                    loads[0].wait()
                    loads[1].wait()
                gate_up(f, c)
    sent([key for key in outward if key != ("s", NF - 1)])
    from_sibling(NF - 1)
    gate_up(NF - 1, other)
    for q in range(4):
        mine = pl.ds(q * PLANE, PLANE)
        gate = acc[mine, :HID]
        hid[mine] = (gate / (1.0 + jnp.exp(-gate)) * acc[mine, HID:]).astype(BF16)

    for load in loads[2:]:
        load.wait()
    sent(list(outward))

    inner, outer = pl.ds(PLANE, 2 * PLANE), pl.ds(3 * PLANE, PLANE)
    first = pl.ds(0, PLANE)

    def down(f, h, dst, parts):
        for mine in parts:
            dst[mine] = mm(hid[mine], wd[f][h]).astype(BF16)

    def down_both(f):
        scratch = rows[f].at[0]
        down(f, other, scratch, (inner,))
        send(("d", f), ("da", f), scratch.at[inner], sib[f].at[inner], dev(dc=1), scratch)
        down(f, c, part[f], (inner,))
        down(f, other, scratch, (outer, first))
        send(("d", f), ("db", f), scratch.at[outer], sib[f].at[outer], dev(dc=1), scratch)
        send(("d", f), ("db", f), scratch.at[first], sib[f].at[first], dev(dc=1), scratch)
        down(f, c, part[f], (outer, first))

    def both(f, mine):
        part[f][mine] = (part[f][mine].astype(F32) + sib[f][mine].astype(F32)).astype(BF16)

    def leave(f):
        arrive(("da", f), sib[f].at[inner])
        both(f, inner)
        for d, q, place in ((-1, 1, 1), (1, 2, 0)):
            send(
                ("xb", f), ("xb", f), part[f].at[pl.ds(q * PLANE, PLANE)], xback[f].at[place], dev(dx=d), xback[f]
            )

    def leave_opposite(f):
        arrive(("db", f), sib[f].at[inner])
        both(f, outer)
        both(f, first)

    def back(p, f):
        for d in (1, 2, 3):
            send(
                ("yb", p, f), ("yb", p, f), part[f].at[pl.ds(base(p) + d * ROWS, ROWS)],
                yback[f].at[p, pl.ds((d - 1) * ROWS, ROWS)], dev(dy=-d), yback[f].at[p],
            )

    def home(f):
        arrive(("xb", f), xback[f])
        total = part[f][first].astype(F32) + xback[f][0].astype(F32) + xback[f][1].astype(F32)
        part[f][first] = total.astype(BF16)
        back(0, f)

    def combine(p, f):
        arrive(("yb", p, f), yback[f].at[p])
        total = mm(mix[p, :, :ROWS], part[f][base(p):base(p) + ROWS])
        total += mm(mix[p, :, ROWS:], yback[f][p])
        zpart[f][p] = total.astype(BF16).reshape(NZ, PAD, WIDTHS[f])
        for s, j, place in ((-1, 3, 0), (1, 5, 1), (-2 if f % 2 == 0 else 2, 4, 2)):
            send(("zi", p, f), ("zi", p, f), zpart[f].at[p, j], zfar[f].at[p, place], dev(dz=s), zfar[f].at[p])

    def closer(p, f):
        def home_by(s, j, place):
            send(("zn", p, f), ("zn", p, f), zpart[f].at[p, j], znear[f].at[p, place], dev(dz=s), znear[f].at[p])

        home_by(-1, 1, 0)
        home_by(1, 7, 1)
        arrive(("zi", p, f), zfar[f].at[p])
        two = zpart[f][p, 2].astype(F32) + zfar[f][p, 0].astype(F32)
        six = zpart[f][p, 6].astype(F32) + zfar[f][p, 1].astype(F32)
        if f % 2 == 0:
            two += zfar[f][p, 2].astype(F32)
        else:
            six += zfar[f][p, 2].astype(F32)
        zpart[f][p, 2] = two.astype(BF16)
        zpart[f][p, 6] = six.astype(BF16)
        home_by(-2, 2, 2)
        home_by(2, 6, 3)

    def gathered(p, f):
        arrive(("zn", p, f), znear[f].at[p])
        total = zpart[f][p, 0].astype(F32)
        for i in range(4):
            total += znear[f][p, i].astype(F32)
        return total

    def opposite(f):
        opp[f][0] = gathered(1, f).astype(BF16)
        send(("ob", f), ("ob", f), opp[f].at[0], opp[f].at[1], dev(dx=2), opp[f].at[0])

    def finish(f):
        total = gathered(0, f)
        arrive(("ob", f), opp[f].at[0])
        total += opp[f][1].astype(F32)
        mine = pl.ds(STARTS[f], WIDTHS[f])
        out[:, mine] = total.astype(BF16)
        results.append(pltpu.make_async_copy(out.at[:, mine], out_hbm.at[:, mine], osem.at[f]))
        results[-1].start()

    down_both(0)
    down_both(1)
    leave(0)
    down_both(2)
    leave_opposite(0)
    leave(1)
    back(1, 0)
    down_both(3)
    leave_opposite(1)
    leave(2)
    leave_opposite(2)
    back(1, 1)
    leave(3)
    back(1, 2)
    down_both(4)
    leave_opposite(3)
    down_both(5)
    back(1, 3)
    home(0)
    leave(4)
    leave_opposite(4)
    leave(5)
    back(1, 4)
    combine(1, 0)
    leave_opposite(5)
    back(1, 5)
    combine(1, 1)
    closer(1, 0)
    home(1)
    combine(1, 2)
    closer(1, 1)
    opposite(0)
    combine(1, 3)
    closer(1, 2)
    home(2)
    combine(0, 0)
    opposite(1)
    closer(1, 3)
    combine(1, 4)
    combine(1, 5)
    opposite(2)
    closer(0, 0)
    home(3)
    combine(0, 1)
    opposite(3)
    closer(1, 4)
    closer(1, 5)
    combine(0, 2)
    home(4)
    closer(0, 1)
    opposite(4)
    home(5)
    opposite(5)
    combine(0, 3)
    finish(0)
    closer(0, 2)
    combine(0, 4)
    finish(1)
    combine(0, 5)
    closer(0, 3)
    finish(2)
    closer(0, 4)
    closer(0, 5)
    finish(3)
    finish(4)
    finish(5)
    sent(list(outward))
    for copy in results:
        copy.wait()


def per_device(tokens, routes, route_weights, w_gate, w_up, w_down):
    half = tokens.shape[1]
    hbm = pl.BlockSpec(memory_space=pl.ANY)

    def chunked(*lead):
        return [pltpu.VMEM((*lead, width), BF16) for width in WIDTHS]

    result = pl.pallas_call(
        kernel,
        out_shape=jax.ShapeDtypeStruct((PAD, half), BF16),
        in_specs=[hbm] * 6,
        out_specs=hbm,
        scratch_shapes=[
            pltpu.VMEM((TOK, half), BF16),
            pltpu.VMEM((TOP, TOK), jnp.int32),
            pltpu.VMEM((TOP, TOK), F32),
            pltpu.VMEM((PAD, half), BF16),
            chunked(2, NZ, PAD),
            pltpu.VMEM((2, NZ, PAD, COLS), BF16),
            pltpu.VMEM((2, PLANE, NZ * PAD), BF16),
            pltpu.VMEM((2, NZ * PAD, PLANE), BF16),
            chunked(2, 3, ROWS),
            chunked(2, 4 * PLANE),
            pltpu.VMEM((2 * half, HID), BF16),
            pltpu.VMEM((2 * half, HID), BF16),
            chunked(2, HID),
            pltpu.VMEM((4 * PLANE, 2 * HID), F32),
            pltpu.VMEM((4 * PLANE, HID), BF16),
            chunked(4 * PLANE),
            chunked(4 * PLANE),
            chunked(2, PLANE),
            chunked(2, 3 * ROWS),
            chunked(2, NZ, PAD),
            chunked(2, 3, PAD),
            chunked(2, 4, PAD),
            chunked(2, PAD),
            pltpu.SemaphoreType.DMA((3,)),
            pltpu.SemaphoreType.DMA((NF,)),
            pltpu.SemaphoreType.DMA((2 + 2 * NF,)),
            pltpu.SemaphoreType.DMA((5 + 9 * NF,)),
            pltpu.SemaphoreType.DMA((5 + 19 * NF,)),
        ],
        compiler_params=pltpu.CompilerParams(
            collective_id=0, has_side_effects=True, vmem_limit_bytes=60 * 1024 * 1024
        ),
        name="experts",
    )(tokens, routes.T, route_weights.T, w_gate, w_up, w_down)
    return result[:TOK]


def solution(mesh):
    placed = (
        P(("attn", "exp"), "rep"),
        P(("attn", "exp"), None),
        P(("attn", "exp"), None),
        P("exp", None, ("attn", "rep")),
        P("exp", None, ("attn", "rep")),
        P("exp", ("attn", "rep"), None),
    )
    return jax.shard_map(
        per_device, mesh=mesh, in_specs=placed, out_specs=P(("attn", "exp"), "rep"), check_vma=False
    )
```

time: 131 us -> 109 us (0.83)
  Pallas kernels: 126 us -> 107 us
  local copies, waits for them, and re-layouts: 4.28 us -> 1.55 us
    pallas_call x1, Pallas kernels: 126 us -> 107 us  [per_device(): pl.pallas_call(kernel, out_shape=jax.ShapeDtypeStruct((PAD, half), BF16),...]
    unnamed x3 -> x1, local copies, waits for them, and re-layouts: 4.28 us -> 1.55 us
where the time goes in v2:
time: 109 us
  Pallas kernels  107 us (98%)
  local copies, waits for them, and re-layouts  1.55 us (1%)
    pallas_call x1, Pallas kernels, per_device(): pl.pallas_call(kernel, out_shape=jax.ShapeDtypeStruct((PAD, half), BF16),...  107 us

profile of v2, /device:TPU:32, one launch (start us, length us, event | category | flops | bytes accessed | tf_op | source)
XLA Modules:
  0.0 109.0 jit_solution(14860114930987171861)
XLA Ops:
  0.0 107.5 %experts.1 = bf16[16,3584]{1,0:T(8,128)(2,1)} custom-call(bf16[12,3584]{1,0:T(8,128)(2,1)} %tokens_hbm.1, s32[8,12]{1,0:T(8,128)} %bitcast.4, f32[8,12]{1,0:T(8,128)} %bitcast.5, bf16[1,7168,256]{2,1,0:T(8,128)(2,1)} %wg_hbm.1, bf16[1,7168,256]{2,1,0:T(8,128)(2,1)} %wu_hbm.1, bf16[1,256,7168]{2,1,0:T(8,128)(2,1)} %wd_hbm.1), custom_call_target="tpu_custom_call" | custom-call | tf_op jit(solution)/shard_map/experts/pallas_call | solution.py:439
  107.5 1.6 %copy.8 = bf16[12,3584]{1,0:T(8,128)(2,1)} copy(bf16[12,3584]{1,0:T(8,128)(2,1)} %bitcast.3) | data formatting | bytes 172032

commit v3 on v2

--- a/solution.py
+++ b/solution.py
@@ -34,7 +34,7 @@
 def kernel(
     tokens_hbm, routes_hbm, weights_hbm, wg_hbm, wu_hbm, wd_hbm, out_hbm,
     tokens, routes, weights, out, tok, tm, pick, mix, ysend, rows, wg, wu, wd, acc, hid,
-    part, sib, xback, yback, zpart, zfar, znear, opp,
+    part, xback, yback, zpart, zfar, znear, zlast, opp,
     isem, osem, wsem, ssem, rsem,
 ):
     half = tokens.shape[1]
@@ -53,7 +53,7 @@
 
     partners = [dev(dx=1), dev(dx=-1), dev(dx=2), dev(dc=1)]
     partners += [dev(dy=d) for d in (1, 2, 3)]
-    partners += [dev(dz=d) for d in (1, -1, 2, -2)]
+    partners += [dev(dz=d) for d in (1, -1, 2, -2, 3, -3, 4)]
     barrier = pltpu.get_barrier_semaphore()
     for partner in partners:
         pl.semaphore_signal(barrier, inc=1, device_id=partner, device_id_type=MESH)
@@ -68,43 +68,45 @@
         pltpu.make_async_copy(wg_hbm.at[0], wg, wsem.at[0]),
         pltpu.make_async_copy(wu_hbm.at[0], wu, wsem.at[1]),
     ]
-    for h in range(2):
-        for f in range(NF):
-            loads.append(
-                pltpu.make_async_copy(
-                    wd_hbm.at[0, :, pl.ds(h * half + STARTS[f], WIDTHS[f])], wd[f].at[h], wsem.at[2 + h * NF + f]
-                )
-            )
-    for load in loads:
-        load.start()
-    for copy in inputs:
-        copy.wait()
+    for f in range(NF):
+        mine = pl.ds(pl.multiple_of(c * half + STARTS[f], 128), WIDTHS[f])
+        loads.append(pltpu.make_async_copy(wd_hbm.at[0, :, mine], wd[f].at[pl.ds(0, HID)], wsem.at[2]))
+    narrow = wg.at[pl.ds(0, half)]
 
     eye = (iota((PAD, TOK), 0) == iota((PAD, TOK), 1)).astype(F32).astype(BF16)
-    for f in range(NF):
+
+    def placement():
+        col = iota((TOK, COLS), 1)
+        expert = sixth(col)
+        slot = col - CAP * expert
+        square = (iota((TOK, TOK), 0) == iota((TOK, TOK), 1)).astype(F32).astype(BF16)
+        names = mm(square, routes[...].astype(F32).astype(BF16), ((1,), (1,))).astype(jnp.int32)
+        gains = mm(square, weights[...].astype(BF16), ((1,), (1,)))
+        hit = jnp.zeros((TOK, COLS), F32)
+        weight = jnp.zeros((TOK, COLS), F32)
+        for k in range(TOP):
+            named = names[:, k:k + 1] == expert
+            hit = jnp.where(named, 1.0, hit)
+            weight = jnp.where(named, gains[:, k:k + 1], weight)
+        lower = (iota((TOK, TOK), 0) > iota((TOK, TOK), 1)).astype(F32).astype(BF16)
+        before = mm(lower, hit.astype(BF16))
+        placed = jnp.where(before == slot.astype(F32), weight, 0.0)
+        tm[0, 0] = mm(eye, placed.astype(BF16)).astype(BF16)
+
+    def padded(f):
         tok[f][0, 0] = mm(eye, tokens[:, STARTS[f]:STARTS[f] + WIDTHS[f]]).astype(BF16)
-    col = iota((TOK, COLS), 1)
-    expert = sixth(col)
-    slot = col - CAP * expert
-    square = (iota((TOK, TOK), 0) == iota((TOK, TOK), 1)).astype(F32).astype(BF16)
-    names = mm(square, routes[...].astype(F32).astype(BF16), ((1,), (1,))).astype(jnp.int32)
-    gains = mm(square, weights[...].astype(BF16), ((1,), (1,)))
-    hit = jnp.zeros((TOK, COLS), F32)
-    weight = jnp.zeros((TOK, COLS), F32)
-    for k in range(TOP):
-        named = names[:, k:k + 1] == expert
-        hit = jnp.where(named, 1.0, hit)
-        weight = jnp.where(named, gains[:, k:k + 1], weight)
-    lower = (iota((TOK, TOK), 0) > iota((TOK, TOK), 1)).astype(F32).astype(BF16)
-    before = mm(lower, hit.astype(BF16))
-    placed = jnp.where(before == slot.astype(F32), weight, 0.0)
-    tm[0, 0] = mm(eye, placed.astype(BF16)).astype(BF16)
+
+    inputs[1].wait()
+    inputs[2].wait()
+    placement()
+    inputs[0].wait()
+    padded(0)
+    padded(1)
 
     pl.semaphore_wait(barrier, len(partners))
 
     inward, outward, whole = {}, {}, {}
     free = list(range(ssem.shape[0]))
-    results = []
 
     def send(out_key, in_key, src, dst, where, block):
         if in_key not in inward:
@@ -130,7 +132,7 @@
         for key in keys:
             slot = outward.pop(key)
             waiter(whole[key], slot, 0).wait_send()
-            free.append(slot)
+            free.insert(0, slot)
 
     hops = ((1, 1, "b"), (-1, 7, "b"), (2, 2, "a"), (-2, 6, "a"))
 
@@ -175,12 +177,21 @@
     def base(p):
         return 0 if p == 0 else 3 * PLANE
 
+    def sideways(f, start, size):
+        for d, q in ((1, 1), (-1, 2)):
+            send(
+                ("x", f), ("x", f), rows[f].at[c, pl.ds(start, size)],
+                rows[f].at[c, pl.ds(q * PLANE + start, size)], dev(dx=d), rows[f].at[c, pl.ds(PLANE, 2 * PLANE)],
+            )
+
     def choose(p, f):
         if f == 0:
             matrices(p)
         arrive(("zb", p, f), tok[f].at[p, pl.ds(0, 5)])
         got = mm(pick[p], tok[f][p].reshape(NZ * PAD, WIDTHS[f])).astype(BF16)
         rows[f][c, base(p):base(p) + ROWS] = got[:ROWS]
+        if p == 0:
+            sideways(f, 0, ROWS)
         for d in (1, 2, 3):
             ysend[f][p, d - 1] = got[d * ROWS:(d + 1) * ROWS]
             send(
@@ -198,10 +209,7 @@
     def onward(p, f):
         arrive(("y", p, f), rows[f].at[c, pl.ds(base(p) + ROWS, 3 * ROWS)])
         if p == 0:
-            block = rows[f].at[c, pl.ds(0, PLANE)]
-            both_ways = rows[f].at[c, pl.ds(PLANE, 2 * PLANE)]
-            send(("x", f), ("x", f), block, rows[f].at[c, pl.ds(PLANE, PLANE)], dev(dx=1), both_ways)
-            send(("x", f), ("x", f), block, rows[f].at[c, pl.ds(2 * PLANE, PLANE)], dev(dx=-1), both_ways)
+            sideways(f, ROWS, PLANE - ROWS)
         to_sibling(f, base(p), PLANE)
 
     def neighbours(f):
@@ -219,10 +227,17 @@
     items = [(p, f) for p in range(2) for f in range(NF)]
     near(*items[0])
     send(("o", 0), ("om", 0), tm.at[0, 0], tm.at[1, 0], dev(dx=2), tm.at[0, 0])
+    near(*items[1])
     for f in range(NF):
-        send(("oz", f), ("oz", f), tok[f].at[0, 0], tok[f].at[1, 0], dev(dx=2), tok[f].at[0, 0])
+        if f > 1:
+            padded(f)
+        send(("oz",), ("oz",), tok[f].at[0, 0], tok[f].at[1, 0], dev(dx=2), out)
+    for load in loads:
+        load.start()
+    for f in range(NF):
+        theirs = pl.ds(pl.multiple_of(other * half + STARTS[f], 128), WIDTHS[f])
+        send(("w",), ("w",), wd_hbm.at[0, :, theirs], wd[f].at[pl.ds(HID, HID)], dev(dc=1), narrow)
     acc[...] = jnp.zeros_like(acc)
-    near(*items[1])
 
     def further(step):
         if step < len(items):
@@ -233,17 +248,22 @@
                 if p == 1:
                     if f == 0:
                         arrive(("om", 0), tm.at[0, 0])
-                    arrive(("oz", f), tok[f].at[0, 0])
+                        arrive(("oz",), out)
                 near(p, f)
 
     further(0)
     further(1)
     for step in range(len(items) + 2):
         if step < len(items):
-            further(step + 2)
+            if step > 0:
+                further(step + 2)
             choose(*items[step])
+            if step == 0:
+                further(2)
         if step >= 2:
             p, f = items[step - 2]
+            if p == 1:
+                sent([("z", 0, f), ("zf", 0, f), ("y", 0, f)])
             if p == 1 and f > 0:
                 from_sibling(f - 1)
                 gate_up(f - 1, other)
@@ -257,47 +277,34 @@
     sent([key for key in outward if key != ("s", NF - 1)])
     from_sibling(NF - 1)
     gate_up(NF - 1, other)
-    for q in range(4):
-        mine = pl.ds(q * PLANE, PLANE)
-        gate = acc[mine, :HID]
-        hid[mine] = (gate / (1.0 + jnp.exp(-gate)) * acc[mine, HID:]).astype(BF16)
-
-    for load in loads[2:]:
-        load.wait()
-    sent(list(outward))
-
     inner, outer = pl.ds(PLANE, 2 * PLANE), pl.ds(3 * PLANE, PLANE)
     first = pl.ds(0, PLANE)
-
-    def down(f, h, dst, parts):
-        for mine in parts:
-            dst[mine] = mm(hid[mine], wd[f][h]).astype(BF16)
-
-    def down_both(f):
-        scratch = rows[f].at[0]
-        down(f, other, scratch, (inner,))
-        send(("d", f), ("da", f), scratch.at[inner], sib[f].at[inner], dev(dc=1), scratch)
-        down(f, c, part[f], (inner,))
-        down(f, other, scratch, (outer, first))
-        send(("d", f), ("db", f), scratch.at[outer], sib[f].at[outer], dev(dc=1), scratch)
-        send(("d", f), ("db", f), scratch.at[first], sib[f].at[first], dev(dc=1), scratch)
-        down(f, c, part[f], (outer, first))
-
-    def both(f, mine):
-        part[f][mine] = (part[f][mine].astype(F32) + sib[f][mine].astype(F32)).astype(BF16)
+    ours, theirs = pl.ds(0, HID), pl.ds(HID, HID)
+    for key, mine in (("inner", inner), ("edge", outer), ("edge", first)):
+        gate = acc[mine, :HID]
+        hid[mine, ours] = (gate / (1.0 + jnp.exp(-gate)) * acc[mine, HID:]).astype(BF16)
+        send(("h",), ("h", key), hid.at[mine, ours], hid.at[mine, theirs], dev(dc=1), hid.at[:, ours])
+
+    sent([key for key in outward if key != ("h",)])
+    pltpu.make_async_copy(narrow, narrow, wsem.at[2]).wait()
+    arrive(("w",), narrow)
+    arrive(("h", "inner"), hid.at[inner, theirs])
+
+    def down(f, mine):
+        part[f][mine] = mm(hid[mine], wd[f][...]).astype(BF16)
 
     def leave(f):
-        arrive(("da", f), sib[f].at[inner])
-        both(f, inner)
+        down(f, inner)
         for d, q, place in ((-1, 1, 1), (1, 2, 0)):
             send(
                 ("xb", f), ("xb", f), part[f].at[pl.ds(q * PLANE, PLANE)], xback[f].at[place], dev(dx=d), xback[f]
             )
 
     def leave_opposite(f):
-        arrive(("db", f), sib[f].at[inner])
-        both(f, outer)
-        both(f, first)
+        if f == 0:
+            arrive(("h", "edge"), hid.at[inner, theirs])
+        down(f, outer)
+        down(f, first)
 
     def back(p, f):
         for d in (1, 2, 3):
@@ -317,6 +324,10 @@
         total = mm(mix[p, :, :ROWS], part[f][base(p):base(p) + ROWS])
         total += mm(mix[p, :, ROWS:], yback[f][p])
         zpart[f][p] = total.astype(BF16).reshape(NZ, PAD, WIDTHS[f])
+        if (p, f) == (0, NF - 1):
+            for j in range(1, NZ):
+                send(("zi", p, f), ("zi", p, f), zpart[f].at[p, j], zlast.at[j - 1], dev(dz=-j), zlast)
+            return
         for s, j, place in ((-1, 3, 0), (1, 5, 1), (-2 if f % 2 == 0 else 2, 4, 2)):
             send(("zi", p, f), ("zi", p, f), zpart[f].at[p, j], zfar[f].at[p, place], dev(dz=s), zfar[f].at[p])
 
@@ -350,83 +361,80 @@
         send(("ob", f), ("ob", f), opp[f].at[0], opp[f].at[1], dev(dx=2), opp[f].at[0])
 
     def finish(f):
-        total = gathered(0, f)
+        if f < NF - 1:
+            total = gathered(0, f)
+        else:
+            arrive(("zi", 0, f), zlast)
+            total = zpart[f][0, 0].astype(F32)
+            for i in range(NZ - 1):
+                total += zlast[i].astype(F32)
         arrive(("ob", f), opp[f].at[0])
         total += opp[f][1].astype(F32)
         mine = pl.ds(STARTS[f], WIDTHS[f])
         out[:, mine] = total.astype(BF16)
-        results.append(pltpu.make_async_copy(out.at[:, mine], out_hbm.at[:, mine], osem.at[f]))
-        results[-1].start()
-
-    down_both(0)
-    down_both(1)
+        pltpu.make_async_copy(out.at[:, mine], out_hbm.at[:, mine], osem.at[0]).start()
+
     leave(0)
-    down_both(2)
     leave_opposite(0)
+    back(1, 0)
     leave(1)
-    back(1, 0)
-    down_both(3)
     leave_opposite(1)
+    back(1, 1)
     leave(2)
     leave_opposite(2)
-    back(1, 1)
     leave(3)
     back(1, 2)
-    down_both(4)
     leave_opposite(3)
-    down_both(5)
-    back(1, 3)
-    home(0)
     leave(4)
     leave_opposite(4)
     leave(5)
-    back(1, 4)
+    leave_opposite(5)
     combine(1, 0)
-    leave_opposite(5)
-    back(1, 5)
+    home(0)
+    back(1, 3)
     combine(1, 1)
     closer(1, 0)
-    home(1)
     combine(1, 2)
     closer(1, 1)
+    home(1)
+    back(1, 4)
     opposite(0)
+    combine(0, 0)
+    closer(1, 2)
+    opposite(1)
     combine(1, 3)
-    closer(1, 2)
+    closer(0, 0)
     home(2)
-    combine(0, 0)
-    opposite(1)
+    back(1, 5)
+    opposite(2)
+    combine(0, 1)
     closer(1, 3)
     combine(1, 4)
+    closer(0, 1)
+    home(3)
+    opposite(3)
+    combine(0, 2)
+    closer(1, 4)
     combine(1, 5)
-    opposite(2)
-    closer(0, 0)
-    home(3)
-    combine(0, 1)
-    opposite(3)
-    closer(1, 4)
-    closer(1, 5)
-    combine(0, 2)
     home(4)
-    closer(0, 1)
+    closer(0, 2)
     opposite(4)
     home(5)
+    combine(0, 3)
+    closer(1, 5)
+    combine(0, 4)
+    finish(0)
+    finish(1)
+    closer(0, 3)
+    combine(0, 5)
     opposite(5)
-    combine(0, 3)
-    finish(0)
-    closer(0, 2)
-    combine(0, 4)
-    finish(1)
-    combine(0, 5)
-    closer(0, 3)
     finish(2)
     closer(0, 4)
-    closer(0, 5)
     finish(3)
+    finish(5)
     finish(4)
-    finish(5)
     sent(list(outward))
-    for copy in results:
-        copy.wait()
+    pltpu.make_async_copy(out, out_hbm, osem.at[0]).wait()
 
 
 def per_device(tokens, routes, route_weights, w_gate, w_up, w_down):
@@ -454,22 +462,22 @@
             chunked(2, 4 * PLANE),
             pltpu.VMEM((2 * half, HID), BF16),
             pltpu.VMEM((2 * half, HID), BF16),
-            chunked(2, HID),
+            chunked(2 * HID),
             pltpu.VMEM((4 * PLANE, 2 * HID), F32),
-            pltpu.VMEM((4 * PLANE, HID), BF16),
-            chunked(4 * PLANE),
+            pltpu.VMEM((4 * PLANE, 2 * HID), BF16),
             chunked(4 * PLANE),
             chunked(2, PLANE),
             chunked(2, 3 * ROWS),
             chunked(2, NZ, PAD),
             chunked(2, 3, PAD),
             chunked(2, 4, PAD),
+            pltpu.VMEM((NZ - 1, PAD, WIDTHS[-1]), BF16),
             chunked(2, PAD),
             pltpu.SemaphoreType.DMA((3,)),
-            pltpu.SemaphoreType.DMA((NF,)),
-            pltpu.SemaphoreType.DMA((2 + 2 * NF,)),
-            pltpu.SemaphoreType.DMA((5 + 9 * NF,)),
-            pltpu.SemaphoreType.DMA((5 + 19 * NF,)),
+            pltpu.SemaphoreType.DMA((1,)),
+            pltpu.SemaphoreType.DMA((3,)),
+            pltpu.SemaphoreType.DMA((51,)),
+            pltpu.SemaphoreType.DMA((104,)),
         ],
         compiler_params=pltpu.CompilerParams(
             collective_id=0, has_side_effects=True, vmem_limit_bytes=60 * 1024 * 1024

time: 109 us -> 105 us (0.963)
  Pallas kernels: 107 us -> 104 us
    pallas_call x1, Pallas kernels: 107 us -> 104 us  [per_device(): pl.pallas_call(kernel, out_shape=jax.ShapeDtypeStruct((PAD, half), BF16),...]
where the time goes in v3:
time: 105 us
  Pallas kernels  104 us (99%)
  local copies, waits for them, and re-layouts  1.55 us (1%)
    pallas_call x1, Pallas kernels, per_device(): pl.pallas_call(kernel, out_shape=jax.ShapeDtypeStruct((PAD, half), BF16),...  104 us

profile of v3, /device:TPU:32, one launch (start us, length us, event | category | flops | bytes accessed | tf_op | source)
XLA Modules:
  0.0 105.1 jit_solution(4994754681560133378)
XLA Ops:
  0.0 103.5 %experts.1 = bf16[16,3584]{1,0:T(8,128)(2,1)} custom-call(bf16[12,3584]{1,0:T(8,128)(2,1)} %tokens_hbm.1, s32[8,12]{1,0:T(8,128)} %bitcast.4, f32[8,12]{1,0:T(8,128)} %bitcast.5, bf16[1,7168,256]{2,1,0:T(8,128)(2,1)} %wg_hbm.1, bf16[1,7168,256]{2,1,0:T(8,128)(2,1)} %wu_hbm.1, bf16[1,256,7168]{2,1,0:T(8,128)(2,1)} %wd_hbm.1), custom_call_target="tpu_custom_call" | custom-call | tf_op jit(solution)/shard_map/experts/pallas_call | solution.py:447
  103.5 1.6 %copy.8 = bf16[12,3584]{1,0:T(8,128)(2,1)} copy(bf16[12,3584]{1,0:T(8,128)(2,1)} %bitcast.3) | data formatting | bytes 172032

commit v4 on v3

--- a/solution.py
+++ b/solution.py
@@ -264,9 +264,6 @@
             p, f = items[step - 2]
             if p == 1:
                 sent([("z", 0, f), ("zf", 0, f), ("y", 0, f)])
-            if p == 1 and f > 0:
-                from_sibling(f - 1)
-                gate_up(f - 1, other)
             onward(p, f)
             if p == 1:
                 neighbours(f)
@@ -274,6 +271,9 @@
                     loads[0].wait()
                     loads[1].wait()
                 gate_up(f, c)
+                if f > 0:
+                    from_sibling(f - 1)
+                    gate_up(f - 1, other)
     sent([key for key in outward if key != ("s", NF - 1)])
     from_sibling(NF - 1)
     gate_up(NF - 1, other)
@@ -375,61 +375,61 @@
         pltpu.make_async_copy(out.at[:, mine], out_hbm.at[:, mine], osem.at[0]).start()
 
     leave(0)
+    leave(1)
     leave_opposite(0)
+    leave(2)
     back(1, 0)
-    leave(1)
+    leave(3)
     leave_opposite(1)
     back(1, 1)
-    leave(2)
+    leave_opposite(3)
     leave_opposite(2)
-    leave(3)
+    leave(4)
     back(1, 2)
-    leave_opposite(3)
-    leave(4)
-    leave_opposite(4)
+    combine(1, 0)
     leave(5)
+    back(1, 3)
+    home(0)
     leave_opposite(5)
-    combine(1, 0)
-    home(0)
-    back(1, 3)
     combine(1, 1)
-    closer(1, 0)
     combine(1, 2)
     closer(1, 1)
+    closer(1, 0)
     home(1)
+    combine(1, 3)
+    back(1, 5)
+    closer(1, 2)
+    combine(0, 0)
+    home(2)
+    closer(1, 3)
+    leave_opposite(4)
     back(1, 4)
-    opposite(0)
-    combine(0, 0)
-    closer(1, 2)
-    opposite(1)
-    combine(1, 3)
-    closer(0, 0)
-    home(2)
-    back(1, 5)
+    combine(1, 5)
     opposite(2)
     combine(0, 1)
-    closer(1, 3)
+    home(3)
+    combine(0, 2)
+    closer(0, 0)
     combine(1, 4)
     closer(0, 1)
-    home(3)
-    opposite(3)
-    combine(0, 2)
+    home(4)
+    closer(1, 5)
+    opposite(0)
+    closer(0, 2)
+    home(5)
+    opposite(1)
+    combine(0, 3)
     closer(1, 4)
-    combine(1, 5)
-    home(4)
-    closer(0, 2)
-    opposite(4)
-    home(5)
-    combine(0, 3)
-    closer(1, 5)
     combine(0, 4)
     finish(0)
+    opposite(3)
+    opposite(5)
+    combine(0, 5)
     finish(1)
     closer(0, 3)
-    combine(0, 5)
-    opposite(5)
     finish(2)
     closer(0, 4)
+    opposite(4)
     finish(3)
     finish(5)
     finish(4)

time: 105 us -> 102 us (0.971)
  Pallas kernels: 104 us -> 99.8 us
    pallas_call x1, Pallas kernels: 104 us -> 99.8 us  [per_device(): pl.pallas_call(kernel, out_shape=jax.ShapeDtypeStruct((PAD, half), BF16),...]
where the time goes in v4:
time: 102 us; the launch traced here: 101 us
  Pallas kernels  99.8 us (98%)
  local copies, waits for them, and re-layouts  1.55 us (2%)
    pallas_call x1, Pallas kernels, per_device(): pl.pallas_call(kernel, out_shape=jax.ShapeDtypeStruct((PAD, half), BF16),...  99.8 us

profile of v4, /device:TPU:32, one launch (start us, length us, event | category | flops | bytes accessed | tf_op | source)
XLA Modules:
  0.0 101.4 jit_solution(16587473462530180656)
XLA Ops:
  0.0 99.8 %experts.1 = bf16[16,3584]{1,0:T(8,128)(2,1)} custom-call(bf16[12,3584]{1,0:T(8,128)(2,1)} %tokens_hbm.1, s32[8,12]{1,0:T(8,128)} %bitcast.4, f32[8,12]{1,0:T(8,128)} %bitcast.5, bf16[1,7168,256]{2,1,0:T(8,128)(2,1)} %wg_hbm.1, bf16[1,7168,256]{2,1,0:T(8,128)(2,1)} %wu_hbm.1, bf16[1,256,7168]{2,1,0:T(8,128)(2,1)} %wd_hbm.1), custom_call_target="tpu_custom_call" | custom-call | tf_op jit(solution)/shard_map/experts/pallas_call | solution.py:447
  99.8 1.6 %copy.8 = bf16[12,3584]{1,0:T(8,128)(2,1)} copy(bf16[12,3584]{1,0:T(8,128)(2,1)} %bitcast.3) | data formatting | bytes 172032

commit v5 on v4

--- a/solution.py
+++ b/solution.py
@@ -32,10 +32,10 @@
 
 
 def kernel(
-    tokens_hbm, routes_hbm, weights_hbm, wg_hbm, wu_hbm, wd_hbm, out_hbm,
-    tokens, routes, weights, out, tok, tm, pick, mix, ysend, rows, wg, wu, wd, acc, hid,
+    tokens_hbm, routes_hbm, weights_hbm, wg_hbm, wu_hbm, wd_hbm, out,
+    tokens, routes, weights, tok, tm, pick, mix, ysend, rows, wg, wu, wd, acc, hid,
     part, xback, yback, zpart, zfar, znear, zlast, opp,
-    isem, osem, wsem, ssem, rsem,
+    isem, wsem, ssem, rsem,
 ):
     half = tokens.shape[1]
     x = lax.axis_index("attn")
@@ -242,7 +242,7 @@
     def further(step):
         if step < len(items):
             far(*items[step])
-        for later in (2, 3) if step == 0 else (step + 3,):
+        for later in {0: (2,), 1: (3, 4)}.get(step, (step + 3,)):
             if later < len(items):
                 p, f = items[later]
                 if p == 1:
@@ -372,7 +372,6 @@
         total += opp[f][1].astype(F32)
         mine = pl.ds(STARTS[f], WIDTHS[f])
         out[:, mine] = total.astype(BF16)
-        pltpu.make_async_copy(out.at[:, mine], out_hbm.at[:, mine], osem.at[0]).start()
 
     leave(0)
     leave(1)
@@ -434,7 +433,6 @@
     finish(5)
     finish(4)
     sent(list(outward))
-    pltpu.make_async_copy(out, out_hbm, osem.at[0]).wait()
 
 
 def per_device(tokens, routes, route_weights, w_gate, w_up, w_down):
@@ -446,14 +444,13 @@
 
     result = pl.pallas_call(
         kernel,
-        out_shape=jax.ShapeDtypeStruct((PAD, half), BF16),
+        out_shape=pltpu.VMEM((PAD, half), BF16),
         in_specs=[hbm] * 6,
-        out_specs=hbm,
+        out_specs=pl.BlockSpec(memory_space=pltpu.VMEM),
         scratch_shapes=[
             pltpu.VMEM((TOK, half), BF16),
             pltpu.VMEM((TOP, TOK), jnp.int32),
             pltpu.VMEM((TOP, TOK), F32),
-            pltpu.VMEM((PAD, half), BF16),
             chunked(2, NZ, PAD),
             pltpu.VMEM((2, NZ, PAD, COLS), BF16),
             pltpu.VMEM((2, PLANE, NZ * PAD), BF16),
@@ -474,7 +471,6 @@
             pltpu.VMEM((NZ - 1, PAD, WIDTHS[-1]), BF16),
             chunked(2, PAD),
             pltpu.SemaphoreType.DMA((3,)),
-            pltpu.SemaphoreType.DMA((1,)),
             pltpu.SemaphoreType.DMA((3,)),
             pltpu.SemaphoreType.DMA((51,)),
             pltpu.SemaphoreType.DMA((104,)),

time: 102 us -> 100 us (0.980)
  no operation moved by 1% of the time
where the time goes in v5:
time: 100 us; the launch traced here: 99.8 us
  Pallas kernels  99.2 us (99%)
    pallas_call x1, Pallas kernels, per_device(): pl.pallas_call(kernel, out_shape=pltpu.VMEM((PAD, half), BF16), in_specs=...  99.2 us

profile of v5, /device:TPU:32, one launch (start us, length us, event | category | flops | bytes accessed | tf_op | source)
XLA Modules:
  0.0 99.8 jit_solution(14429914190165444195)
XLA Ops:
  0.0 99.2 %experts.1 = bf16[16,3584]{1,0:T(8,128)(2,1)S(1)} custom-call(bf16[12,3584]{1,0:T(8,128)(2,1)} %tokens_hbm.1, s32[8,12]{1,0:T(8,128)} %bitcast.4, f32[8,12]{1,0:T(8,128)} %bitcast.5, bf16[1,7168,256]{2,1,0:T(8,128)(2,1)} %wg_hbm.1, bf16[1,7168,256]{2,1,0:T(8,128)(2,1)} %wu_hbm.1, bf16[1,256,7168]{2,1,0:T(8,128)(2,1)} %wd_hbm.1), custom_call_target="tpu_custom_call" | custom-call | tf_op jit(solution)/shard_map/experts/pallas_call | solution.py:445
  99.2 0.6 copy.8

commit v6 on v5

--- a/solution.py
+++ b/solution.py
@@ -101,7 +101,6 @@
     placement()
     inputs[0].wait()
     padded(0)
-    padded(1)
 
     pl.semaphore_wait(barrier, len(partners))
 
@@ -139,23 +138,23 @@
     def near(p, f):
         if f == 0:
             for s, j, part_of in hops:
-                send(("m", p), ("m" + part_of, p), tm.at[p, 0], tm.at[p, j], dev(dz=s), tm.at[p, pl.ds(0, 4)])
+                send(("m", p), ("m" + part_of, p), tm.at[p, 0], tm.at[p, j], dev(dz=s), tm.at[p, pl.ds(0, 7)])
         for s, j, part_of in hops:
             send(
                 ("z", p, f), ("z" + part_of, p, f), tok[f].at[p, 0], tok[f].at[p, j], dev(dz=s),
-                tok[f].at[p, pl.ds(0, 4)],
+                tok[f].at[p, pl.ds(0, 7)],
             )
 
     def far(p, f):
         if f == 0:
             arrive(("ma", p), tm.at[p, pl.ds(0, 2)])
             for s, i, j in ((1, 2, 3), (-1, 6, 5), (2, 2, 4)):
-                send(("mf", p), ("mb", p), tm.at[p, i], tm.at[p, j], dev(dz=s), tm.at[p, pl.ds(0, 3)])
+                send(("m", p), ("mb", p), tm.at[p, i], tm.at[p, j], dev(dz=s), tm.at[p, pl.ds(0, 7)])
         arrive(("za", p, f), tok[f].at[p, pl.ds(0, 2)])
         for s, i, j in ((1, 2, 3), (-1, 6, 5), (2, 2, 4) if f % 2 == 0 else (-2, 6, 4)):
             send(
-                ("zf", p, f), ("zb", p, f), tok[f].at[p, i], tok[f].at[p, j], dev(dz=s),
-                tok[f].at[p, pl.ds(0, 3)],
+                ("z", p, f), ("zb", p, f), tok[f].at[p, i], tok[f].at[p, j], dev(dz=s),
+                tok[f].at[p, pl.ds(0, 7)],
             )
 
     def matrices(p):
@@ -227,6 +226,7 @@
     items = [(p, f) for p in range(2) for f in range(NF)]
     near(*items[0])
     send(("o", 0), ("om", 0), tm.at[0, 0], tm.at[1, 0], dev(dx=2), tm.at[0, 0])
+    padded(1)
     near(*items[1])
     for f in range(NF):
         if f > 1:
@@ -263,7 +263,7 @@
         if step >= 2:
             p, f = items[step - 2]
             if p == 1:
-                sent([("z", 0, f), ("zf", 0, f), ("y", 0, f)])
+                sent([("z", 0, f), ("y", 0, f)])
             onward(p, f)
             if p == 1:
                 neighbours(f)
@@ -472,7 +472,7 @@
             chunked(2, PAD),
             pltpu.SemaphoreType.DMA((3,)),
             pltpu.SemaphoreType.DMA((3,)),
-            pltpu.SemaphoreType.DMA((51,)),
+            pltpu.SemaphoreType.DMA((48,)),
             pltpu.SemaphoreType.DMA((104,)),
         ],
         compiler_params=pltpu.CompilerParams(

time: 100 us -> 100 us (level)
  no operation moved by 1% of the time
where the time goes in v6:
time: 100 us; the launch traced here: 99.7 us
  Pallas kernels  99.1 us (99%)
    pallas_call x1, Pallas kernels, per_device(): pl.pallas_call(kernel, out_shape=pltpu.VMEM((PAD, half), BF16), in_specs=...  99.1 us

profile of v6, /device:TPU:32, one launch (start us, length us, event | category | flops | bytes accessed | tf_op | source)
XLA Modules:
  0.0 99.7 jit_solution(3298313563569327519)
XLA Ops:
  0.0 99.1 %experts.1 = bf16[16,3584]{1,0:T(8,128)(2,1)S(1)} custom-call(bf16[12,3584]{1,0:T(8,128)(2,1)} %tokens_hbm.1, s32[8,12]{1,0:T(8,128)} %bitcast.4, f32[8,12]{1,0:T(8,128)} %bitcast.5, bf16[1,7168,256]{2,1,0:T(8,128)(2,1)} %wg_hbm.1, bf16[1,7168,256]{2,1,0:T(8,128)(2,1)} %wu_hbm.1, bf16[1,256,7168]{2,1,0:T(8,128)(2,1)} %wd_hbm.1), custom_call_target="tpu_custom_call" | custom-call | tf_op jit(solution)/shard_map/experts/pallas_call | solution.py:445
  99.1 0.6 copy.8
